TPU v7x, 512 devices: a whole 4x8x8 slice. The times are simulated.
512 devices in a mesh: tm: 16 (over y, core), clus: 32 (over z, x).
Axes of the slice: x: 4, y: 8, z: 8, core: 2. Of those that a mesh axis runs over, the one named last changes fastest.
Arguments:
- series: bfloat16 [65536, 1024], P(('clus', 'tm')), parts along dimension 0, may hold values from -11 to 11
- block_time: int32 [1024], P('clus'), parts along dimension 0, may hold values from 0 to 31, each once
- w_qkv: bfloat16 [1024, 3072], replicated, may hold values from -0.1875 to 0.1875
- w_out: bfloat16 [1024, 1024], replicated, may hold values from -0.1875 to 0.1875
Outputs:
- result: bfloat16 [65536, 1024], P(('clus', 'tm')), parts along dimension 0
There are 32 independent parts, one for each index of `clus`. A program takes and returns all parts, laid end to end along the dimension named above; an argument that names none is the same for every part. Nothing has to cross between parts.
Inputs may be any that keep to these rules, and one draw needn't show every extreme that they name: block_time is a permutation of the stored blocks' time indices.
All inputs are finite; a program needn't handle non-finite values.
Results may differ from a plain program's by a relative error of at most 0.012.
The roundings to bfloat16 on the way count: a program that leaves them out, or rounds other values in their place, can miss the bound.
Values may be sent and summed in bfloat16 or wider, within the bound.
No kernel may reach another device: no remote copies, remote signals or barrier semaphores. Data moves between devices by JAX's collectives and lax.ppermute only.
A program may use at most 128 MiB of HBM per device.

v0:
```python
import jax
import jax.numpy as jnp
from jax import lax
from jax.sharding import PartitionSpec as P

HEADS = 16


def shifted(block, axis, distance):
    devices = range(lax.axis_size(axis))
    route = [((i - distance) % len(devices), i) for i in devices]
    return lax.ppermute(block, axis, route)


def positions(block_time, owner, width):
    pair = lax.dynamic_slice_in_dim(block_time, 2 * owner, 2)
    return (pair[:, None] * width + jnp.arange(width, dtype=jnp.int32)[None, :]).reshape(-1)


def empty_state(heads, rows, size):
    return (
        jnp.full((heads, rows), -1e30, jnp.float32),
        jnp.zeros((heads, rows), jnp.float32),
        jnp.zeros((rows, heads, size), jnp.float32),
    )


def panel_update(state, queries, panel, qtime, ktime, heads):
    top, total, summed = state
    rows, width = queries.shape
    krows = panel.shape[0]
    size = width // heads
    keys = panel[:, :width].reshape(krows, heads, size)
    values = panel[:, width:].reshape(krows, heads, size)
    scores = (
        jnp.einsum(
            "lhe,mhe->hlm",
            queries.reshape(rows, heads, size),
            keys,
            preferred_element_type=jnp.float32,
        )
        * 0.125
    )
    keep = ktime[None, None, :] <= qtime[None, :, None]
    newtop = jnp.maximum(top, jnp.max(jnp.where(keep, scores, -1e30), axis=-1))
    probs = jnp.where(keep, jnp.exp(scores - newtop[:, :, None]), 0.0)
    factor = jnp.exp(top - newtop)
    total = total * factor + jnp.sum(probs, axis=-1)
    added = jnp.einsum(
        "hlm,mhe->lhe", probs.astype(jnp.bfloat16), values, preferred_element_type=jnp.float32
    )
    return (newtop, total, summed * factor.T[:, :, None] + added)


def guarded(state, queries, panel, qtime, ktime, heads):
    return panel_update(state, queries, panel, qtime, ktime, heads)


def shards(series, block_time, w_qkv, w_out):
    rows, width = series.shape
    heads = HEADS
    size = width // heads
    blocks = rows // 2
    count = lax.axis_size("tm")
    index = lax.axis_index("tm")
    qkv = jnp.dot(series, w_qkv, preferred_element_type=jnp.float32).astype(jnp.bfloat16)
    queries = qkv[:, :width]
    panel = qkv[:, width:]
    qtime = positions(block_time, index, blocks)
    state = guarded(empty_state(heads, rows, size), queries, panel, qtime, qtime, heads)
    moving = panel
    for step in range(1, count):
        moving = shifted(moving, "tm", 1)
        ktime = positions(block_time, (index - step) % count, blocks)
        state = guarded(state, queries, moving, qtime, ktime, heads)
    attended = (state[2] / state[1].T[:, :, None]).reshape(rows, width).astype(jnp.bfloat16)
    mixed = series.astype(jnp.float32) + jnp.dot(
        attended, w_out, preferred_element_type=jnp.float32
    )
    return mixed.astype(jnp.bfloat16)


def solution(mesh):
    placed = (P(("clus", "tm"), None), P("clus"), P(), P())
    return jax.shard_map(
        shards, mesh=mesh, in_specs=placed, out_specs=P(("clus", "tm"), None), check_vma=False
    )
```

profile of v0, /device:TPU:1, one launch (start us, length us, event | category | flops | bytes accessed | tf_op | source)
XLA Modules:
  0.0 212.7 jit_solution(1998495715751271881)
XLA Ops:
  0.0 4.0 %convolution_convert_fusion = bf16[128,3072]{1,0:T(8,128)(2,1)S(1)} fusion(bf16[128,1024]{1,0:T(8,128)(2,1)} %param.4, bf16[1024,3072]{1,0:T(8,128)(2,1)} %param.6), kind=kOutput, calls=%fused_computation | convolution fusion | flops 805699584 | bytes 7340032 | tf_op jit(solution)/shard_map/dot_general | solution.py:66
  4.1 2.7 %collective-permute-start = (bf16[128,2048]{1,0:T(8,128)(2,1)S(1)}, bf16[128,2048]{1,0:T(8,128)(2,1)}, u32[]{:S(2)}, u32[]{:S(2)}) collective-permute-start(bf16[128,2048]{1,0:T(8,128)(2,1)S(1)} %slice.141), channel_id=1, source_target_pairs={{480,0},{0,32},{32,64},{64,96},{96,128},{128,160},{160,192},{192,2... | collective-permute-start | bytes 1572872 | tf_op jit(solution)/shard_map/ppermute | solution.py:12
  6.8 6.1 %collective-permute-done = bf16[128,2048]{1,0:T(8,128)(2,1)} collective-permute-done((bf16[128,2048]{1,0:T(8,128)(2,1)S(1)}, bf16[128,2048]{1,0:T(8,128)(2,1)}, u32[]{:S(2)}, u32[]{:S(2)}) %collective-permute-start) | collective-permute-done | bytes 524320 | tf_op jit(solution)/shard_map/ppermute | solution.py:12
  12.9 2.6 %collective-permute-start.1 = (bf16[128,2048]{1,0:T(8,128)(2,1)}, bf16[128,2048]{1,0:T(8,128)(2,1)S(1)}, u32[]{:S(2)}, u32[]{:S(2)}) collective-permute-start(bf16[128,2048]{1,0:T(8,128)(2,1)} %collective-permute-done), channel_id=1, source_target_pairs={{480,0},{0,32},{32,64},{64,96},{96,128},{128,160},{160,192},{192,2... | collective-permute-start | bytes 1572872 | tf_op jit(solution)/shard_map/ppermute | solution.py:12
  15.7 6.8 %collective-permute-done.1 = bf16[128,2048]{1,0:T(8,128)(2,1)S(1)} collective-permute-done((bf16[128,2048]{1,0:T(8,128)(2,1)}, bf16[128,2048]{1,0:T(8,128)(2,1)S(1)}, u32[]{:S(2)}, u32[]{:S(2)}) %collective-permute-start.1) | collective-permute-done | bytes 524320 | tf_op jit(solution)/shard_map/ppermute | solution.py:12
  24.5 7.8 %collective-permute-done.2 = bf16[128,2048]{1,0:T(8,128)(2,1)S(1)} collective-permute-done((bf16[128,2048]{1,0:T(8,128)(2,1)S(1)}, bf16[128,2048]{1,0:T(8,128)(2,1)S(1)}, u32[]{:S(2)}, u32[]{:S(2)}) %collective-permute-start.2) | collective-permute-done | bytes 524320 | tf_op jit(solution)/shard_map/ppermute | solution.py:12
  33.9 9.1 %collective-permute-done.3 = bf16[128,2048]{1,0:T(8,128)(2,1)} collective-permute-done((bf16[128,2048]{1,0:T(8,128)(2,1)S(1)}, bf16[128,2048]{1,0:T(8,128)(2,1)}, u32[]{:S(2)}, u32[]{:S(2)}) %collective-permute-start.3) | collective-permute-done | bytes 524320 | tf_op jit(solution)/shard_map/ppermute | solution.py:12
  57.9 1.9 select_reduce_fusion.15
  63.4 1.9 select_reduce_fusion.14
  65.4 2.7 %collective-permute-done.5 = bf16[128,2048]{1,0:T(8,128)(2,1)} collective-permute-done((bf16[128,2048]{1,0:T(8,128)(2,1)}, bf16[128,2048]{1,0:T(8,128)(2,1)}, u32[]{:S(2)}, u32[]{:S(2)}) %collective-permute-start.5) | collective-permute-done | bytes 524320 | tf_op jit(solution)/shard_map/ppermute | solution.py:12
  68.0 1.9 fusion.183
  73.5 2.9 %select_reduce_fusion.13 = (f32[16,128]{1,0:T(8,128)}, f32[16,128,128]{1,2,0:T(8,128)}) fusion(pred[128,128]{0,1:T(8,128)(4,1)} %get-tuple-element.77, bf16[128,16,64]{0,2,1:T(8,128)(2,1)S(1)} %bitcast.405, bf16[128,16,64]{0,2,1:T(8,128)(2,1)} %bitcast.442), kind=kOutput, calls=%fused_computation.95 | convolution fusion | flops 34338816 | bytes 1597440 | tf_op jit(solution)/shard_map/lhe,mhe->hlm/dot_general | solution.py:36
  80.0 2.9 %select_reduce_fusion.12 = (f32[16,128]{1,0:T(8,128)}, f32[16,128,128]{1,2,0:T(8,128)}) fusion(pred[128,128]{0,1:T(8,128)(4,1)} %get-tuple-element.78, bf16[128,16,64]{0,2,1:T(8,128)(2,1)S(1)} %bitcast.406, bf16[128,16,64]{0,2,1:T(8,128)(2,1)} %bitcast.437), kind=kOutput, calls=%fused_computation.93 | convolution fusion | flops 34338816 | bytes 1597440 | tf_op jit(solution)/shard_map/lhe,mhe->hlm/dot_general | solution.py:36
  84.7 1.9 fusion.181
  90.2 2.9 %select_reduce_fusion.11 = (f32[16,128]{1,0:T(8,128)}, f32[16,128,128]{1,2,0:T(8,128)}) fusion(pred[128,128]{0,1:T(8,128)(4,1)} %get-tuple-element.79, bf16[128,16,64]{0,2,1:T(8,128)(2,1)S(1)} %bitcast.407, bf16[128,16,64]{0,2,1:T(8,128)(2,1)} %bitcast.443), kind=kOutput, calls=%fused_computation.91 | convolution fusion | flops 34338816 | bytes 1597440 | tf_op jit(solution)/shard_map/lhe,mhe->hlm/dot_general | solution.py:36
  98.5 2.9 %select_reduce_fusion.10 = (f32[16,128]{1,0:T(8,128)}, f32[16,128,128]{1,2,0:T(8,128)}) fusion(pred[128,128]{0,1:T(8,128)(4,1)} %get-tuple-element.80, bf16[128,16,64]{0,2,1:T(8,128)(2,1)S(1)} %bitcast.408, bf16[128,16,64]{0,2,1:T(8,128)(2,1)} %bitcast.444), kind=kOutput, calls=%fused_computation.89 | convolution fusion | flops 34338816 | bytes 1597440 | tf_op jit(solution)/shard_map/lhe,mhe->hlm/dot_general | solution.py:36
  101.4 1.9 fusion.179
  105.1 3.9 %collective-permute-start.9 = (bf16[128,2048]{1,0:T(8,128)(2,1)}, bf16[128,2048]{1,0:T(8,128)(2,1)}, u32[]{:S(2)}, u32[]{:S(2)}) collective-permute-start(bf16[128,2048]{1,0:T(8,128)(2,1)} %collective-permute-done.8), channel_id=1, source_target_pairs={{480,0},{0,32},{32,64},{64,96},{96,128},{128,160},{160,192},{192,2... | collective-permute-start | bytes 1572872 | tf_op jit(solution)/shard_map/ppermute | solution.py:12
  109.0 2.9 %select_reduce_fusion.9 = (f32[16,128]{1,0:T(8,128)}, f32[16,128,128]{1,2,0:T(8,128)}) fusion(pred[128,128]{0,1:T(8,128)(4,1)S(1)} %get-tuple-element.81, bf16[128,16,64]{0,2,1:T(8,128)(2,1)S(1)} %bitcast.409, bf16[128,16,64]{0,2,1:T(8,128)(2,1)} %bitcast.438), kind=kOutput, calls=%fused_computation.87 | convolution fusion | flops 34338816 | bytes 1597440 | tf_op jit(solution)/shard_map/lhe,mhe->hlm/dot_general | solution.py:36
  119.2 2.9 %select_reduce_fusion.8 = (f32[16,128]{1,0:T(8,128)}, f32[16,128,128]{1,2,0:T(8,128)}) fusion(pred[128,128]{0,1:T(8,128)(4,1)S(1)} %get-tuple-element.82, bf16[128,16,64]{0,2,1:T(8,128)(2,1)S(1)} %bitcast.410, bf16[128,16,64]{0,2,1:T(8,128)(2,1)} %bitcast.445), kind=kOutput, calls=%fused_computation.85 | convolution fusion | flops 34338816 | bytes 1597440 | tf_op jit(solution)/shard_map/lhe,mhe->hlm/dot_general | solution.py:36
  122.1 3.8 %collective-permute-start.10 = (bf16[128,2048]{1,0:T(8,128)(2,1)}, bf16[128,2048]{1,0:T(8,128)(2,1)}, u32[]{:S(2)}, u32[]{:S(2)}) collective-permute-start(bf16[128,2048]{1,0:T(8,128)(2,1)} %collective-permute-done.9), channel_id=1, source_target_pairs={{480,0},{0,32},{32,64},{64,96},{96,128},{128,160},{160,192},{192,2... | collective-permute-start | bytes 1572872 | tf_op jit(solution)/shard_map/ppermute | solution.py:12
  125.9 1.9 fusion.177
  131.4 3.0 %select_reduce_fusion.7 = (f32[16,128]{1,0:T(8,128)}, f32[16,128,128]{1,2,0:T(8,128)}) fusion(pred[128,128]{0,1:T(8,128)(4,1)S(1)} %get-tuple-element.83, bf16[128,16,64]{0,2,1:T(8,128)(2,1)S(1)} %bitcast.411, bf16[128,16,64]{0,2,1:T(8,128)(2,1)} %bitcast.446), kind=kOutput, calls=%fused_computation.83 | convolution fusion | flops 34338816 | bytes 1597440 | tf_op jit(solution)/shard_map/lhe,mhe->hlm/dot_general | solution.py:36
  134.3 1.9 fusion.176
  138.0 2.9 %select_reduce_fusion.6 = (f32[16,128]{1,0:T(8,128)}, f32[16,128,128]{1,2,0:T(8,128)}) fusion(pred[128,128]{0,1:T(8,128)(4,1)S(1)} %get-tuple-element.84, bf16[128,16,64]{0,2,1:T(8,128)(2,1)S(1)} %bitcast.412, bf16[128,16,64]{0,2,1:T(8,128)(2,1)} %bitcast.439), kind=kOutput, calls=%fused_computation.81 | convolution fusion | flops 34338816 | bytes 1597440 | tf_op jit(solution)/shard_map/lhe,mhe->hlm/dot_general | solution.py:36
  148.2 2.9 %select_reduce_fusion.5 = (f32[16,128]{1,0:T(8,128)}, f32[16,128,128]{1,2,0:T(8,128)}) fusion(pred[128,128]{0,1:T(8,128)(4,1)S(1)} %get-tuple-element.85, bf16[128,16,64]{0,2,1:T(8,128)(2,1)S(1)} %bitcast.413, bf16[128,16,64]{0,2,1:T(8,128)(2,1)} %bitcast.447), kind=kOutput, calls=%fused_computation.79 | convolution fusion | flops 34338816 | bytes 1597440 | tf_op jit(solution)/shard_map/lhe,mhe->hlm/dot_general | solution.py:36
  151.1 2.7 %collective-permute-start.12 = (bf16[128,2048]{1,0:T(8,128)(2,1)}, bf16[128,2048]{1,0:T(8,128)(2,1)}, u32[]{:S(2)}, u32[]{:S(2)}) collective-permute-start(bf16[128,2048]{1,0:T(8,128)(2,1)} %collective-permute-done.11), channel_id=1, source_target_pairs={{480,0},{0,32},{32,64},{64,96},{96,128},{128,160},{160,192},{192,2... | collective-permute-start | bytes 1572872 | tf_op jit(solution)/shard_map/ppermute | solution.py:12
  159.2 2.9 %select_reduce_fusion.4 = (f32[16,128]{1,0:T(8,128)}, f32[16,128,128]{1,2,0:T(8,128)}) fusion(pred[128,128]{0,1:T(8,128)(4,1)S(1)} %get-tuple-element.86, bf16[128,16,64]{0,2,1:T(8,128)(2,1)S(1)} %bitcast.414, bf16[128,16,64]{0,2,1:T(8,128)(2,1)} %bitcast.448), kind=kOutput, calls=%fused_computation.77 | convolution fusion | flops 34338816 | bytes 1597440 | tf_op jit(solution)/shard_map/lhe,mhe->hlm/dot_general | solution.py:36
  165.8 2.9 %select_reduce_fusion.3 = (f32[16,128]{1,0:T(8,128)}, f32[16,128,128]{1,2,0:T(8,128)}) fusion(pred[128,128]{0,1:T(8,128)(4,1)S(1)} %get-tuple-element.87, bf16[128,16,64]{0,2,1:T(8,128)(2,1)S(1)} %bitcast.415, bf16[128,16,64]{0,2,1:T(8,128)(2,1)} %bitcast.435), kind=kOutput, calls=%fused_computation.75 | convolution fusion | flops 34338816 | bytes 1597440 | tf_op jit(solution)/shard_map/lhe,mhe->hlm/dot_general | solution.py:36
  172.0 1.9 fusion.172
  175.7 2.9 %select_reduce_fusion.2 = (f32[16,128]{1,0:T(8,128)}, f32[16,128,128]{1,2,0:T(8,128)}) fusion(pred[128,128]{0,1:T(8,128)(4,1)S(1)} %get-tuple-element.88, bf16[128,16,64]{0,2,1:T(8,128)(2,1)S(1)} %bitcast.416, bf16[128,16,64]{0,2,1:T(8,128)(2,1)} %bitcast.436), kind=kOutput, calls=%fused_computation.73 | convolution fusion | flops 34338816 | bytes 1597440 | tf_op jit(solution)/shard_map/lhe,mhe->hlm/dot_general | solution.py:36
  185.8 2.9 %select_reduce_fusion.1 = (f32[16,128]{1,0:T(8,128)}, f32[16,128,128]{1,2,0:T(8,128)}) fusion(pred[128,128]{0,1:T(8,128)(4,1)S(1)} %get-tuple-element.89, bf16[128,16,64]{0,2,1:T(8,128)(2,1)S(1)} %bitcast.417, bf16[128,16,64]{0,2,1:T(8,128)(2,1)} %bitcast.449), kind=kOutput, calls=%fused_computation.71 | convolution fusion | flops 34338816 | bytes 1597440 | tf_op jit(solution)/shard_map/lhe,mhe->hlm/dot_general | solution.py:36
  (247 shorter events, 106.8 us)
Async XLA Ops:
  0.0 211.1 %copy-start = (bf16[1024,1024]{1,0:T(8,128)(2,1)S(1)}, bf16[1024,1024]{1,0:T(8,128)(2,1)}, u32[]{:S(2)}) copy-start(bf16[1024,1024]{1,0:T(8,128)(2,1)} %param.7) | copy-start | bytes 6291460
  0.0 15.5 %copy-start.49 = (s32[32]{0:T(128)S(1)}, s32[32]{0:T(128)}, u32[]{:S(2)}) copy-start(s32[32]{0:T(128)} %param.5) | copy-start | bytes 388
  4.1 8.8 %collective-permute-start = (bf16[128,2048]{1,0:T(8,128)(2,1)S(1)}, bf16[128,2048]{1,0:T(8,128)(2,1)}, u32[]{:S(2)}, u32[]{:S(2)}) collective-permute-start(bf16[128,2048]{1,0:T(8,128)(2,1)S(1)} %slice.141), channel_id=1, source_target_pairs={{480,0},{0,32},{32,64},{64,96},{96,128},{128,160},{160,192},{192,2... | collective-permute-start | bytes 1572872 | tf_op jit(solution)/shard_map/ppermute | solution.py:12
  12.9 9.6 %collective-permute-start.1 = (bf16[128,2048]{1,0:T(8,128)(2,1)}, bf16[128,2048]{1,0:T(8,128)(2,1)S(1)}, u32[]{:S(2)}, u32[]{:S(2)}) collective-permute-start(bf16[128,2048]{1,0:T(8,128)(2,1)} %collective-permute-done), channel_id=1, source_target_pairs={{480,0},{0,32},{32,64},{64,96},{96,128},{128,160},{160,192},{192,2... | collective-permute-start | bytes 1572872 | tf_op jit(solution)/shard_map/ppermute | solution.py:12
  22.5 29.9 %copy-start.31 = (bf16[128,2048]{1,0:T(8,128)(2,1)}, bf16[128,2048]{1,0:T(8,128)(2,1)S(1)}, u32[]{:S(2)}) copy-start(bf16[128,2048]{1,0:T(8,128)(2,1)S(1)} %collective-permute-done.1) | copy-start | bytes 1572868
  22.5 9.8 %collective-permute-start.2 = (bf16[128,2048]{1,0:T(8,128)(2,1)S(1)}, bf16[128,2048]{1,0:T(8,128)(2,1)S(1)}, u32[]{:S(2)}, u32[]{:S(2)}) collective-permute-start(bf16[128,2048]{1,0:T(8,128)(2,1)S(1)} %collective-permute-done.1), channel_id=1, source_target_pairs={{480,0},{0,32},{32,64},{64,96},{96,128},{128,160},{160,192},{192,2... | collective-permute-start | bytes 1572872 | tf_op jit(solution)/shard_map/ppermute | solution.py:12
  33.1 9.9 %collective-permute-start.3 = (bf16[128,2048]{1,0:T(8,128)(2,1)S(1)}, bf16[128,2048]{1,0:T(8,128)(2,1)}, u32[]{:S(2)}, u32[]{:S(2)}) collective-permute-start(bf16[128,2048]{1,0:T(8,128)(2,1)S(1)} %collective-permute-done.2), channel_id=1, source_target_pairs={{480,0},{0,32},{32,64},{64,96},{96,128},{128,160},{160,192},{192,2... | collective-permute-start | bytes 1572872 | tf_op jit(solution)/shard_map/ppermute | solution.py:12
  43.1 14.8 %collective-permute-start.4 = (bf16[128,2048]{1,0:T(8,128)(2,1)}, bf16[128,2048]{1,0:T(8,128)(2,1)}, u32[]{:S(2)}, u32[]{:S(2)}) collective-permute-start(bf16[128,2048]{1,0:T(8,128)(2,1)} %collective-permute-done.3), channel_id=1, source_target_pairs={{480,0},{0,32},{32,64},{64,96},{96,128},{128,160},{160,192},{192,2... | collective-permute-start | bytes 1572872 | tf_op jit(solution)/shard_map/ppermute | solution.py:12
  57.9 2.0 copy-start.38
  57.9 10.1 %collective-permute-start.5 = (bf16[128,2048]{1,0:T(8,128)(2,1)}, bf16[128,2048]{1,0:T(8,128)(2,1)}, u32[]{:S(2)}, u32[]{:S(2)}) collective-permute-start(bf16[128,2048]{1,0:T(8,128)(2,1)} %collective-permute-done.4), channel_id=1, source_target_pairs={{480,0},{0,32},{32,64},{64,96},{96,128},{128,160},{160,192},{192,2... | collective-permute-start | bytes 1572872 | tf_op jit(solution)/shard_map/ppermute | solution.py:12
  68.0 12.0 %collective-permute-start.6 = (bf16[128,2048]{1,0:T(8,128)(2,1)}, bf16[128,2048]{1,0:T(8,128)(2,1)}, u32[]{:S(2)}, u32[]{:S(2)}) collective-permute-start(bf16[128,2048]{1,0:T(8,128)(2,1)} %collective-permute-done.5), channel_id=1, source_target_pairs={{480,0},{0,32},{32,64},{64,96},{96,128},{128,160},{160,192},{192,2... | collective-permute-start | bytes 1572872 | tf_op jit(solution)/shard_map/ppermute | solution.py:12
  80.0 13.0 %collective-permute-start.7 = (bf16[128,2048]{1,0:T(8,128)(2,1)}, bf16[128,2048]{1,0:T(8,128)(2,1)}, u32[]{:S(2)}, u32[]{:S(2)}) collective-permute-start(bf16[128,2048]{1,0:T(8,128)(2,1)} %collective-permute-done.6), channel_id=1, source_target_pairs={{480,0},{0,32},{32,64},{64,96},{96,128},{128,160},{160,192},{192,2... | collective-permute-start | bytes 1572872 | tf_op jit(solution)/shard_map/ppermute | solution.py:12
  93.0 12.1 %collective-permute-start.8 = (bf16[128,2048]{1,0:T(8,128)(2,1)}, bf16[128,2048]{1,0:T(8,128)(2,1)}, u32[]{:S(2)}, u32[]{:S(2)}) collective-permute-start(bf16[128,2048]{1,0:T(8,128)(2,1)} %collective-permute-done.7), channel_id=1, source_target_pairs={{480,0},{0,32},{32,64},{64,96},{96,128},{128,160},{160,192},{192,2... | collective-permute-start | bytes 1572872 | tf_op jit(solution)/shard_map/ppermute | solution.py:12
  105.1 17.0 %collective-permute-start.9 = (bf16[128,2048]{1,0:T(8,128)(2,1)}, bf16[128,2048]{1,0:T(8,128)(2,1)}, u32[]{:S(2)}, u32[]{:S(2)}) collective-permute-start(bf16[128,2048]{1,0:T(8,128)(2,1)} %collective-permute-done.8), channel_id=1, source_target_pairs={{480,0},{0,32},{32,64},{64,96},{96,128},{128,160},{160,192},{192,2... | collective-permute-start | bytes 1572872 | tf_op jit(solution)/shard_map/ppermute | solution.py:12
  122.1 15.9 %collective-permute-start.10 = (bf16[128,2048]{1,0:T(8,128)(2,1)}, bf16[128,2048]{1,0:T(8,128)(2,1)}, u32[]{:S(2)}, u32[]{:S(2)}) collective-permute-start(bf16[128,2048]{1,0:T(8,128)(2,1)} %collective-permute-done.9), channel_id=1, source_target_pairs={{480,0},{0,32},{32,64},{64,96},{96,128},{128,160},{160,192},{192,2... | collective-permute-start | bytes 1572872 | tf_op jit(solution)/shard_map/ppermute | solution.py:12
  138.0 13.1 %collective-permute-start.11 = (bf16[128,2048]{1,0:T(8,128)(2,1)}, bf16[128,2048]{1,0:T(8,128)(2,1)}, u32[]{:S(2)}, u32[]{:S(2)}) collective-permute-start(bf16[128,2048]{1,0:T(8,128)(2,1)} %collective-permute-done.10), channel_id=1, source_target_pairs={{480,0},{0,32},{32,64},{64,96},{96,128},{128,160},{160,192},{192,2... | collective-permute-start | bytes 1572872 | tf_op jit(solution)/shard_map/ppermute | solution.py:12
  151.1 14.7 %collective-permute-start.12 = (bf16[128,2048]{1,0:T(8,128)(2,1)}, bf16[128,2048]{1,0:T(8,128)(2,1)}, u32[]{:S(2)}, u32[]{:S(2)}) collective-permute-start(bf16[128,2048]{1,0:T(8,128)(2,1)} %collective-permute-done.11), channel_id=1, source_target_pairs={{480,0},{0,32},{32,64},{64,96},{96,128},{128,160},{160,192},{192,2... | collective-permute-start | bytes 1572872 | tf_op jit(solution)/shard_map/ppermute | solution.py:12
  165.8 9.9 %collective-permute-start.13 = (bf16[128,2048]{1,0:T(8,128)(2,1)}, bf16[128,2048]{1,0:T(8,128)(2,1)}, u32[]{:S(2)}, u32[]{:S(2)}) collective-permute-start(bf16[128,2048]{1,0:T(8,128)(2,1)} %collective-permute-done.12), channel_id=1, source_target_pairs={{480,0},{0,32},{32,64},{64,96},{96,128},{128,160},{160,192},{192,2... | collective-permute-start | bytes 1572872 | tf_op jit(solution)/shard_map/ppermute | solution.py:12
  175.7 13.1 %collective-permute-start.14 = (bf16[128,2048]{1,0:T(8,128)(2,1)}, bf16[128,2048]{1,0:T(8,128)(2,1)}, u32[]{:S(2)}, u32[]{:S(2)}) collective-permute-start(bf16[128,2048]{1,0:T(8,128)(2,1)} %collective-permute-done.13), channel_id=1, source_target_pairs={{480,0},{0,32},{32,64},{64,96},{96,128},{128,160},{160,192},{192,2... | collective-permute-start | bytes 1572872 | tf_op jit(solution)/shard_map/ppermute | solution.py:12
  194.2 4.1 %copy-start.37 = (pred[128,128]{0,1:T(8,128)(4,1)S(1)}, pred[128,128]{0,1:T(8,128)(4,1)}, u32[]{:S(2)}) copy-start(pred[128,128]{0,1:T(8,128)(4,1)} %get-tuple-element.92) | copy-start | bytes 49156
  194.2 4.4 %copy-start.1 = (f32[16,128,128]{1,2,0:T(8,128)S(1)}, f32[16,128,128]{1,2,0:T(8,128)}, u32[]{:S(2)}) copy-start(f32[16,128,128]{1,2,0:T(8,128)} %get-tuple-element.136) | copy-start | bytes 3145732
  194.2 4.4 %copy-start.36 = (pred[128,128]{0,1:T(8,128)(4,1)S(1)}, pred[128,128]{0,1:T(8,128)(4,1)}, u32[]{:S(2)}) copy-start(pred[128,128]{0,1:T(8,128)(4,1)} %get-tuple-element.77) | copy-start | bytes 49156
  195.8 3.0 %copy-start.2 = (f32[16,128,128]{1,2,0:T(8,128)S(1)}, f32[16,128,128]{1,2,0:T(8,128)}, u32[]{:S(2)}) copy-start(f32[16,128,128]{1,2,0:T(8,128)} %get-tuple-element.134) | copy-start | bytes 3145732
  195.8 3.0 %copy-start.35 = (pred[128,128]{0,1:T(8,128)(4,1)S(1)}, pred[128,128]{0,1:T(8,128)(4,1)}, u32[]{:S(2)}) copy-start(pred[128,128]{0,1:T(8,128)(4,1)} %get-tuple-element.78) | copy-start | bytes 49156
  196.7 2.2 %copy-start.3 = (f32[16,128,128]{1,2,0:T(8,128)S(1)}, f32[16,128,128]{1,2,0:T(8,128)}, u32[]{:S(2)}) copy-start(f32[16,128,128]{1,2,0:T(8,128)} %get-tuple-element.132) | copy-start | bytes 3145732
  196.8 2.2 %copy-start.34 = (pred[128,128]{0,1:T(8,128)(4,1)S(1)}, pred[128,128]{0,1:T(8,128)(4,1)}, u32[]{:S(2)}) copy-start(pred[128,128]{0,1:T(8,128)(4,1)} %get-tuple-element.79) | copy-start | bytes 49156
  198.8 1.5 copy-start.7
  199.0 1.6 copy-start.8
  199.5 1.4 copy-start.9
  200.3 1.4 copy-start.11
  200.6 1.4 copy-start.12
  201.3 1.4 copy-start.14
  (43 other events, 49.5 us)
where the time goes:
time: 216 us; the launch traced here: 213 us
  local copies, waits for them, and re-layouts  98.9 us (46%)
  matrix products  52.8 us (24%)
  waiting for transfers between devices  32.6 us (15%)
  starting transfers between devices  18.2 us (8%)
  other arithmetic  9.44 us (4%)
    slice x31, local copies, waits for them, and re-layouts, panel_update(): values = panel[:, width:].reshape(krows, heads, size)  54 us
    dot_general x16, matrix products, panel_update(): jnp.einsum('lhe,mhe->hlm', queries.reshape(rows, heads, size), keys, pref...  43.1 us
    ppermute x15, waiting for transfers between devices, shifted(): return lax.ppermute(block, axis, route)  32.6 us
    slice x17, local copies, waits for them, and re-layouts, panel_update(): keys = panel[:, :width].reshape(krows, heads, size)  28 us
    ppermute x15, starting transfers between devices, shifted(): return lax.ppermute(block, axis, route)  18.2 us
    add x16, local copies, waits for them, and re-layouts, positions(): pair[:, None] * width + jnp.arange(width, dtype=jnp.int32)[None, :]  9.88 us
    unnamed x120, local copies, waits for them, and re-layouts  5.92 us
    dot_general x16, matrix products, panel_update(): jnp.einsum('hlm,mhe->lhe', probs.astype(jnp.bfloat16), values, preferred_...  4.5 us
  transfers between devices with their start and end apart: 15, of which 5 were waited for; matrix products, arithmetic and copies ran while one was open for 63% of the time, Pallas kernels for 0%

commit v1 on v0

v1 whole, which is shorter than its diff:
```python
import jax
import jax.numpy as jnp
from jax import lax
from jax.experimental import pallas as pl
from jax.experimental.pallas import tpu as pltpu
from jax.sharding import PartitionSpec as P

HEADS = 16
HEAD = 64
D = 1024
BLK = 64
ROWS = 2 * BLK
N_TM = 16
TOKENS = N_TM * ROWS
TILE = 256
GROUP = 256
NT = (((1,), (1,)), ((), ()))
SCALE = 0.125 * 1.4426950408889634


def swap_halves(tile):
    top, low = tile[:BLK], tile[BLK:]
    first = jnp.concatenate([top[:, :HEAD], low[:, :HEAD]], axis=1)
    second = jnp.concatenate([top[:, HEAD:], low[:, HEAD:]], axis=1)
    return first, second


def project_kernel(x_ref, w_ref, out_ref, w_buf, sem):
    groups = D // GROUP
    copies = []
    for g in range(groups):
        for part in range(3):
            columns = pl.ds(part * D + g * GROUP, GROUP)
            copy = pltpu.make_async_copy(
                w_ref.at[:, columns], w_buf.at[g * 3 + part], sem.at[g * 3 + part]
            )
            copy.start()
            copies.append(copy)
    x = x_ref[...]
    for g in range(groups):
        for part in range(3):
            copies[g * 3 + part].wait()
            y = jnp.dot(x, w_buf[g * 3 + part], preferred_element_type=jnp.float32)
            y = y.astype(jnp.bfloat16)
            for pair in range(GROUP // 128):
                first, second = swap_halves(y[:, pair * 128 : pair * 128 + 128])
                head = g * (GROUP // HEAD) + 2 * pair
                out_ref[head, part * BLK : part * BLK + BLK, :] = first
                out_ref[head + 1, part * BLK : part * BLK + BLK, :] = second


def project(x, w):
    return pl.pallas_call(
        project_kernel,
        out_shape=jax.ShapeDtypeStruct((HEADS, 3 * BLK, ROWS), jnp.bfloat16),
        in_specs=[
            pl.BlockSpec(memory_space=pltpu.VMEM),
            pl.BlockSpec(memory_space=pl.ANY),
        ],
        out_specs=pl.BlockSpec(memory_space=pltpu.VMEM),
        scratch_shapes=[
            pltpu.VMEM((3 * D // GROUP, D, GROUP), jnp.bfloat16),
            pltpu.SemaphoreType.DMA((3 * D // GROUP,)),
        ],
        compiler_params=pltpu.CompilerParams(vmem_limit_bytes=56 * 2**20),
        name="project",
    )(x, w)


def attend_kernel(time_ref, in_ref, out_ref, qs, ks, vs, vt, os):
    for b in range(2 * N_TM):
        source, half = b // 2, b % 2
        rows = pl.ds(pl.multiple_of(time_ref[b] * BLK, BLK), BLK)
        for part, ref in enumerate((qs, ks, vs)):
            ref[rows, :] = in_ref[
                source, part * BLK : part * BLK + BLK, half * HEAD : half * HEAD + HEAD
            ]
    for i in range(TOKENS // TILE):
        span = slice(i * TILE, (i + 1) * TILE)
        vt[:, span] = vs[span, :].T
    before = lax.broadcasted_iota(jnp.int32, (TILE, TILE), 0)
    after = lax.broadcasted_iota(jnp.int32, (TILE, TILE), 1)
    keep = before <= after
    for i in range(TOKENS // TILE):
        span = slice(i * TILE, (i + 1) * TILE)
        q = qs[span, :]
        diagonal = lax.dot_general(ks[span, :], q, NT, preferred_element_type=jnp.float32)
        diagonal = jnp.where(keep, diagonal, -1e30)
        tops = jnp.max(diagonal, axis=0, keepdims=True)
        if i:
            scores = lax.dot_general(
                ks[: i * TILE, :], q, NT, preferred_element_type=jnp.float32
            )
            tops = jnp.maximum(tops, jnp.max(scores, axis=0, keepdims=True))
        probs = jnp.exp2((diagonal - tops) * SCALE)
        total = jnp.sum(probs, axis=0, keepdims=True)
        summed = jnp.dot(
            vt[:, span], probs.astype(jnp.bfloat16), preferred_element_type=jnp.float32
        )
        if i:
            probs = jnp.exp2((scores - tops) * SCALE)
            total = total + jnp.sum(probs, axis=0, keepdims=True)
            summed = summed + jnp.dot(
                vt[:, : i * TILE], probs.astype(jnp.bfloat16), preferred_element_type=jnp.float32
            )
        os[span, :] = (summed / total).astype(jnp.bfloat16).T
    for s in range(N_TM):
        pair = []
        for half in range(2):
            rows = pl.ds(pl.multiple_of(time_ref[2 * s + half] * BLK, BLK), BLK)
            pair.append(os[rows, :])
        out_ref[s] = jnp.concatenate(pair, axis=1)


def attend(block_time, received):
    return pl.pallas_call(
        attend_kernel,
        out_shape=jax.ShapeDtypeStruct((N_TM, BLK, ROWS), jnp.bfloat16),
        in_specs=[
            pl.BlockSpec(memory_space=pltpu.SMEM),
            pl.BlockSpec(memory_space=pltpu.VMEM),
        ],
        out_specs=pl.BlockSpec(memory_space=pltpu.VMEM),
        scratch_shapes=[pltpu.VMEM((TOKENS, HEAD), jnp.bfloat16)] * 3
        + [pltpu.VMEM((HEAD, TOKENS), jnp.bfloat16), pltpu.VMEM((TOKENS, HEAD), jnp.bfloat16)],
        compiler_params=pltpu.CompilerParams(vmem_limit_bytes=32 * 2**20),
        name="attend",
    )(block_time, received)


def mix_kernel(in_ref, x_ref, w_ref, out_ref, rows_ref):
    for pair in range(HEADS // 2):
        first, second = in_ref[2 * pair], in_ref[2 * pair + 1]
        columns = slice(pair * 128, pair * 128 + 128)
        rows_ref[:BLK, columns] = jnp.concatenate([first[:, :HEAD], second[:, :HEAD]], axis=1)
        rows_ref[BLK:, columns] = jnp.concatenate([first[:, HEAD:], second[:, HEAD:]], axis=1)
    mixed = jnp.dot(rows_ref[...], w_ref[...], preferred_element_type=jnp.float32)
    out_ref[...] = (x_ref[...].astype(jnp.float32) + mixed).astype(jnp.bfloat16)


def mix(attended, x, w):
    return pl.pallas_call(
        mix_kernel,
        out_shape=jax.ShapeDtypeStruct((ROWS, D), jnp.bfloat16),
        in_specs=[pl.BlockSpec(memory_space=pltpu.VMEM)] * 3,
        out_specs=pl.BlockSpec(memory_space=pltpu.VMEM),
        scratch_shapes=[pltpu.VMEM((ROWS, D), jnp.bfloat16)],
        compiler_params=pltpu.CompilerParams(vmem_limit_bytes=16 * 2**20),
        name="mix",
    )(attended, x, w)


def shards(series, block_time, w_qkv, w_out):
    sent = project(series, w_qkv)
    received = lax.all_to_all(sent, "tm", 0, 0, tiled=True)
    attended = attend(block_time, received)
    returned = lax.all_to_all(attended, "tm", 0, 0, tiled=True)
    return mix(returned, series, w_out)


def solution(mesh):
    placed = (P(("clus", "tm"), None), P("clus"), P(), P())
    return jax.shard_map(
        shards, mesh=mesh, in_specs=placed, out_specs=P(("clus", "tm"), None), check_vma=False
    )
```

time: 216 us -> 62.6 us (0.29); the launches traced: 213 us -> 62.4 us
  local copies, waits for them, and re-layouts: 98.9 us -> 0.01 us
  matrix products: 52.8 us -> 0 us
  blocking collectives: 0 us -> 47.7 us
  waiting for transfers between devices: 32.6 us -> 0 us
  starting transfers between devices: 18.2 us -> 0 us
  Pallas kernels: 0 us -> 14.7 us
  other arithmetic: 9.44 us -> 0 us
    slice x50 -> x0, local copies, waits for them, and re-layouts: 83.1 us -> none  [the longest x31 54 us: panel_update(): values = panel[:, width:].reshape(krows, heads, size)]
    dot_general x34 -> x0, matrix products: 52.8 us -> none  [the longest x16 43.1 us: panel_update(): jnp.einsum('lhe,mhe->hlm', queries.reshape(rows, heads, size), keys, pref...]
    all_to_all x0 -> x2, blocking collectives: none -> 47.7 us  [the longest x1 33.4 us: shards(): received = lax.all_to_all(sent, 'tm', 0, 0, tiled=True)]
    ppermute x15 -> x0, waiting for transfers between devices: 32.6 us -> none  [shifted(): return lax.ppermute(block, axis, route)]
    ppermute x15 -> x0, starting transfers between devices: 18.2 us -> none  [shifted(): return lax.ppermute(block, axis, route)]
    pallas_call x0 -> x3, Pallas kernels: none -> 14.7 us  [the longest x1 7.44 us: project(): pl.pallas_call(project_kernel, out_shape=jax.ShapeDtypeStruct((HEADS, 3 *...]
    add x16 -> x0, local copies, waits for them, and re-layouts: 9.88 us -> none  [positions(): pair[:, None] * width + jnp.arange(width, dtype=jnp.int32)[None, :]]
    unnamed x120 -> x6, local copies, waits for them, and re-layouts: 5.92 us -> 0.01 us
  transfers between devices with their start and end apart: 15 -> 0, of which waited for: 5 -> 0; matrix products, arithmetic and copies ran while one was open for 63% -> 0% of each run, Pallas kernels for 0% -> 0%
where the time goes in v1:
time: 62.6 us; the launch traced here: 62.4 us
  blocking collectives  47.7 us (76%)
  Pallas kernels  14.7 us (23%)
    all_to_all x1, blocking collectives, shards(): received = lax.all_to_all(sent, 'tm', 0, 0, tiled=True)  33.4 us
    all_to_all x1, blocking collectives, shards(): returned = lax.all_to_all(attended, 'tm', 0, 0, tiled=True)  14.2 us
    pallas_call x1, Pallas kernels, project(): pl.pallas_call(project_kernel, out_shape=jax.ShapeDtypeStruct((HEADS, 3 *...  7.44 us
    pallas_call x1, Pallas kernels, attend(): pl.pallas_call(attend_kernel, out_shape=jax.ShapeDtypeStruct((N_TM, BLK,...  6.05 us

profile of v1, /device:TPU:1, one launch (start us, length us, event | category | flops | bytes accessed | tf_op | source)
XLA Modules:
  0.0 62.4 jit_solution(6353008695449369573)
XLA Ops:
  0.0 0.0 copy-start.1
  0.0 0.0 copy-start.2
  0.0 0.0 copy-start
  0.0 7.4 %project.1 = bf16[16,192,128]{2,1,0:T(8,128)(2,1)} custom-call(bf16[128,1024]{1,0:T(8,128)(2,1)} %x_ref.3, bf16[1024,3072]{1,0:T(8,128)(2,1)} %w_ref.2), custom_call_target="tpu_custom_call" | custom-call | tf_op jit(solution)/shard_map/project/pallas_call | solution.py:53
  7.5 33.4 %all_to_all.10.in_ref = bf16[16,192,128]{2,1,0:T(8,128)(2,1)S(1)} all-to-all(bf16[16,192,128]{2,1,0:T(8,128)(2,1)} %project.1), channel_id=1, replica_groups=mesh['tm'=16,'clus'=32] {'tm'}, dimensions={0} | all-to-all | bytes 1572864 | tf_op jit(solution)/shard_map/all_to_all | solution.py:155
  40.9 0.0 copy-done.2
  40.9 6.1 %attend.1 = bf16[16,64,128]{2,1,0:T(8,128)(2,1)S(1)} custom-call(s32[32]{0:T(128)S(1)} %copy-done.2, bf16[16,192,128]{2,1,0:T(8,128)(2,1)S(1)} %all_to_all.10.in_ref), custom_call_target="tpu_custom_call" | custom-call | tf_op jit(solution)/shard_map/attend/pallas_call | solution.py:116
  47.0 14.2 %all_to_all.11.in_ref = bf16[16,64,128]{2,1,0:T(8,128)(2,1)S(1)} all-to-all(bf16[16,64,128]{2,1,0:T(8,128)(2,1)S(1)} %attend.1), channel_id=1, replica_groups=mesh['tm'=16,'clus'=32] {'tm'}, dimensions={0} | all-to-all | bytes 524288 | tf_op jit(solution)/shard_map/all_to_all | solution.py:157
  61.2 0.0 copy-done.1
  61.2 0.0 copy-done
  61.2 1.2 %mix.1 = bf16[128,1024]{1,0:T(8,128)(2,1)} custom-call(bf16[16,64,128]{2,1,0:T(8,128)(2,1)S(1)} %all_to_all.11.in_ref, bf16[128,1024]{1,0:T(8,128)(2,1)S(1)} %copy-done.1, bf16[1024,1024]{1,0:T(8,128)(2,1)S(1)} %copy-done), custom_call_target="tpu_custom_call" | custom-call | tf_op jit(solution)/shard_map/mix/pallas_call | solution.py:142
Async XLA Ops:
  0.0 61.2 %copy-start.1 = (bf16[128,1024]{1,0:T(8,128)(2,1)S(1)}, bf16[128,1024]{1,0:T(8,128)(2,1)}, u32[]{:S(2)}) copy-start(bf16[128,1024]{1,0:T(8,128)(2,1)} %x_ref.3) | copy-start | bytes 786436
  0.0 40.9 %copy-start.2 = (s32[32]{0:T(128)S(1)}, s32[32]{0:T(128)}, u32[]{:S(2)}) copy-start(s32[32]{0:T(128)} %time_ref.1) | copy-start | bytes 388
  0.0 61.2 %copy-start = (bf16[1024,1024]{1,0:T(8,128)(2,1)S(1)}, bf16[1024,1024]{1,0:T(8,128)(2,1)}, u32[]{:S(2)}) copy-start(bf16[1024,1024]{1,0:T(8,128)(2,1)} %w_ref.3) | copy-start | bytes 6291460

commit v2 on v1

v2 whole, which is shorter than its diff:
```python
import jax
import jax.numpy as jnp
from jax import lax
from jax.experimental import pallas as pl
from jax.experimental.pallas import tpu as pltpu
from jax.sharding import PartitionSpec as P

HEADS = 16
HEAD = 64
D = 1024
BLK = 64
ROWS = 2 * BLK
N_TM = 16
TOKENS = N_TM * ROWS
QTILE = 512
KTILE = 1024
GROUP = 256
CHUNK = 256
PROJECT_VMEM = 52 * 2**20
NT = (((1,), (1,)), ((), ()))
SCALE = 0.125 * 1.4426950408889634


def swap_halves(tile):
    top, low = tile[:BLK], tile[BLK:]
    first = jnp.concatenate([top[:, :HEAD], low[:, :HEAD]], axis=1)
    second = jnp.concatenate([top[:, HEAD:], low[:, HEAD:]], axis=1)
    return first, second


def project_kernel(x_ref, w_ref, out_ref, w_buf, total, sem):
    chunks = D // CHUNK
    copies = []
    for c in range(chunks):
        rows = pl.ds(c * CHUNK, CHUNK)
        copies.append(pltpu.make_async_copy(w_ref.at[rows], w_buf.at[rows], sem.at[c]))
        copies[-1].start()
    for c in range(chunks):
        copies[c].wait()
        depth = slice(c * CHUNK, (c + 1) * CHUNK)
        for g in range(3 * D // GROUP):
            columns = slice(g * GROUP, (g + 1) * GROUP)
            y = jnp.dot(
                x_ref[:, depth], w_buf[depth, columns], preferred_element_type=jnp.float32
            )
            if c:
                y = y + total[:, columns]
            if c < chunks - 1:
                total[:, columns] = y
                continue
            y = y.astype(jnp.bfloat16)
            part, start = g * GROUP // D, g * GROUP % D
            for pair in range(GROUP // 128):
                first, second = swap_halves(y[:, pair * 128 : pair * 128 + 128])
                head = start // HEAD + 2 * pair
                out_ref[head, part * BLK : part * BLK + BLK, :] = first
                out_ref[head + 1, part * BLK : part * BLK + BLK, :] = second


def project(x, w):
    return pl.pallas_call(
        project_kernel,
        out_shape=jax.ShapeDtypeStruct((HEADS, 3 * BLK, ROWS), jnp.bfloat16),
        in_specs=[
            pl.BlockSpec(memory_space=pltpu.VMEM),
            pl.BlockSpec(memory_space=pl.ANY),
        ],
        out_specs=pl.BlockSpec(memory_space=pltpu.VMEM),
        scratch_shapes=[
            pltpu.VMEM((D, 3 * D), jnp.bfloat16),
            pltpu.VMEM((ROWS, 3 * D), jnp.float32),
            pltpu.SemaphoreType.DMA((D // CHUNK,)),
        ],
        compiler_params=pltpu.CompilerParams(vmem_limit_bytes=PROJECT_VMEM),
        name="project",
    )(x, w)


def attend_kernel(time_ref, in_ref, out_ref, qs, ks, vs, os):
    ones = jnp.ones((BLK, HEAD), jnp.bfloat16)
    for b in range(2 * N_TM):
        source, half = b // 2, b % 2
        rows = pl.ds(pl.multiple_of(time_ref[b] * BLK, BLK), BLK)
        columns = slice(half * HEAD, half * HEAD + HEAD)
        qs[rows, :] = in_ref[source, :BLK, columns]
        ks[rows, :] = in_ref[source, BLK : 2 * BLK, columns]
        vs[rows, :] = jnp.concatenate([in_ref[source, 2 * BLK :, columns], ones], axis=1)
    for start in range(0, TOKENS, QTILE):
        q = qs[start : start + QTILE, :]
        top = summed = None
        for first in range(0, start + QTILE, KTILE):
            last = min(first + KTILE, start + QTILE)
            scores = lax.dot_general(q, ks[first:last, :], NT, preferred_element_type=jnp.float32)
            if last > start:
                shape = (QTILE, last - first)
                later = lax.broadcasted_iota(jnp.int32, shape, 0) + start
                earlier = lax.broadcasted_iota(jnp.int32, shape, 1) + first
                scores = jnp.where(earlier <= later, scores, -1e30)
            new_top = jnp.max(scores, axis=1, keepdims=True)
            if top is not None:
                new_top = jnp.maximum(top, new_top)
            probs = jnp.exp2((scores - new_top) * SCALE).astype(jnp.bfloat16)
            added = jnp.dot(probs, vs[first:last, :], preferred_element_type=jnp.float32)
            if top is not None:
                added = summed * jnp.exp2((top - new_top) * SCALE) + added
            top, summed = new_top, added
        os[start : start + QTILE, :] = (summed[:, :HEAD] / summed[:, HEAD:]).astype(jnp.bfloat16)
    for s in range(N_TM):
        pair = []
        for half in range(2):
            rows = pl.ds(pl.multiple_of(time_ref[2 * s + half] * BLK, BLK), BLK)
            pair.append(os[rows, :])
        out_ref[s] = jnp.concatenate(pair, axis=1)


def attend(block_time, received):
    return pl.pallas_call(
        attend_kernel,
        out_shape=jax.ShapeDtypeStruct((N_TM, BLK, ROWS), jnp.bfloat16),
        in_specs=[
            pl.BlockSpec(memory_space=pltpu.SMEM),
            pl.BlockSpec(memory_space=pltpu.VMEM),
        ],
        out_specs=pl.BlockSpec(memory_space=pltpu.VMEM),
        scratch_shapes=[
            pltpu.VMEM((TOKENS, HEAD), jnp.bfloat16),
            pltpu.VMEM((TOKENS, HEAD), jnp.bfloat16),
            pltpu.VMEM((TOKENS, 2 * HEAD), jnp.bfloat16),
            pltpu.VMEM((TOKENS, HEAD), jnp.bfloat16),
        ],
        compiler_params=pltpu.CompilerParams(vmem_limit_bytes=32 * 2**20),
        name="attend",
    )(block_time, received)


def mix_kernel(in_ref, x_ref, w_ref, out_ref, rows_ref):
    for pair in range(HEADS // 2):
        first, second = in_ref[2 * pair], in_ref[2 * pair + 1]
        columns = slice(pair * 128, pair * 128 + 128)
        rows_ref[:BLK, columns] = jnp.concatenate([first[:, :HEAD], second[:, :HEAD]], axis=1)
        rows_ref[BLK:, columns] = jnp.concatenate([first[:, HEAD:], second[:, HEAD:]], axis=1)
    mixed = jnp.dot(rows_ref[...], w_ref[...], preferred_element_type=jnp.float32)
    out_ref[...] = (x_ref[...].astype(jnp.float32) + mixed).astype(jnp.bfloat16)


def mix(attended, x, w):
    return pl.pallas_call(
        mix_kernel,
        out_shape=jax.ShapeDtypeStruct((ROWS, D), jnp.bfloat16),
        in_specs=[pl.BlockSpec(memory_space=pltpu.VMEM)] * 3,
        out_specs=pl.BlockSpec(memory_space=pltpu.VMEM),
        scratch_shapes=[pltpu.VMEM((ROWS, D), jnp.bfloat16)],
        compiler_params=pltpu.CompilerParams(vmem_limit_bytes=16 * 2**20),
        name="mix",
    )(attended, x, w)


def shards(series, block_time, w_qkv, w_out):
    sent = project(series, w_qkv)
    sent, w_out = lax.optimization_barrier((sent, w_out))
    received = lax.all_to_all(sent, "tm", 0, 0, tiled=True)
    attended = attend(block_time, received)
    returned = lax.all_to_all(attended, "tm", 0, 0, tiled=True)
    return mix(returned, series, w_out)


def solution(mesh):
    placed = (P(("clus", "tm"), None), P("clus"), P(), P())
    return jax.shard_map(
        shards, mesh=mesh, in_specs=placed, out_specs=P(("clus", "tm"), None), check_vma=False
    )
```

time: 62.6 us -> 56.9 us (0.909)
  Pallas kernels: 14.7 us -> 8.88 us
  local copies, waits for them, and re-layouts: 0.01 us -> 1.11 us
  blocking collectives: 47.7 us -> 46.7 us
    pallas_call x1, Pallas kernels: 7.44 us -> 3.34 us  [project(): pl.pallas_call(project_kernel, out_shape=jax.ShapeDtypeStruct((HEADS, 3 *...]
    pallas_call x1, Pallas kernels: 6.05 us -> 4.34 us  [attend(): pl.pallas_call(attend_kernel, out_shape=jax.ShapeDtypeStruct((N_TM, BLK,...]
    unnamed x6, local copies, waits for them, and re-layouts: 0.01 us -> 1.11 us
    all_to_all x1, blocking collectives: 33.4 us -> 32.5 us  [shards(): received = lax.all_to_all(sent, 'tm', 0, 0, tiled=True)]
where the time goes in v2:
time: 56.9 us; the launch traced here: 56.7 us
  blocking collectives  46.7 us (82%)
  Pallas kernels  8.88 us (16%)
  local copies, waits for them, and re-layouts  1.11 us (2%)
    all_to_all x1, blocking collectives, shards(): received = lax.all_to_all(sent, 'tm', 0, 0, tiled=True)  32.5 us
    all_to_all x1, blocking collectives, shards(): returned = lax.all_to_all(attended, 'tm', 0, 0, tiled=True)  14.2 us
    pallas_call x1, Pallas kernels, attend(): pl.pallas_call(attend_kernel, out_shape=jax.ShapeDtypeStruct((N_TM, BLK,...  4.34 us
    pallas_call x1, Pallas kernels, project(): pl.pallas_call(project_kernel, out_shape=jax.ShapeDtypeStruct((HEADS, 3 *...  3.34 us
    pallas_call x1, Pallas kernels, mix(): pl.pallas_call(mix_kernel, out_shape=jax.ShapeDtypeStruct((ROWS, D), jnp....  1.2 us

profile of v2, /device:TPU:1, one launch (start us, length us, event | category | flops | bytes accessed | tf_op | source)
XLA Modules:
  0.0 56.7 jit_solution(14087849506733895901)
XLA Ops:
  0.0 0.0 copy-start
  0.0 0.0 copy-start.1
  0.0 1.1 %copy-done.1 = bf16[128,1024]{1,0:T(8,128)(2,1)S(1)} copy-done((bf16[128,1024]{1,0:T(8,128)(2,1)S(1)}, bf16[128,1024]{1,0:T(8,128)(2,1)}, u32[]{:S(2)}) %copy-start.1) | copy-done | bytes 262168
  1.1 0.0 copy-start.2
  1.1 3.3 %project.1 = bf16[16,192,128]{2,1,0:T(8,128)(2,1)S(1)} custom-call(bf16[128,1024]{1,0:T(8,128)(2,1)S(1)} %copy-done.1, bf16[1024,3072]{1,0:T(8,128)(2,1)} %w_ref.1), custom_call_target="tpu_custom_call" | custom-call | tf_op jit(solution)/shard_map/project/pallas_call | solution.py:61
  4.5 32.5 %all_to_all.10.in_ref = bf16[16,192,128]{2,1,0:T(8,128)(2,1)S(1)} all-to-all(bf16[16,192,128]{2,1,0:T(8,128)(2,1)S(1)} %project.1), channel_id=1, replica_groups=mesh['tm'=16,'clus'=32] {'tm'}, dimensions={0} | all-to-all | bytes 1572864 | tf_op jit(solution)/shard_map/all_to_all | solution.py:161
  36.9 0.0 copy-done.2
  36.9 4.3 %attend.1 = bf16[16,64,128]{2,1,0:T(8,128)(2,1)S(1)} custom-call(s32[32]{0:T(128)S(1)} %copy-done.2, bf16[16,192,128]{2,1,0:T(8,128)(2,1)S(1)} %all_to_all.10.in_ref), custom_call_target="tpu_custom_call" | custom-call | tf_op jit(solution)/shard_map/attend/pallas_call | solution.py:117
  41.3 14.2 %all_to_all.11.in_ref = bf16[16,64,128]{2,1,0:T(8,128)(2,1)S(1)} all-to-all(bf16[16,64,128]{2,1,0:T(8,128)(2,1)S(1)} %attend.1), channel_id=1, replica_groups=mesh['tm'=16,'clus'=32] {'tm'}, dimensions={0} | all-to-all | bytes 524288 | tf_op jit(solution)/shard_map/all_to_all | solution.py:163
  55.5 0.0 copy-done
  55.5 1.2 %mix.1 = bf16[128,1024]{1,0:T(8,128)(2,1)} custom-call(bf16[16,64,128]{2,1,0:T(8,128)(2,1)S(1)} %all_to_all.11.in_ref, bf16[128,1024]{1,0:T(8,128)(2,1)S(1)} %copy-done.1, bf16[1024,1024]{1,0:T(8,128)(2,1)S(1)} %copy-done), custom_call_target="tpu_custom_call" | custom-call | tf_op jit(solution)/shard_map/mix/pallas_call | solution.py:147
Async XLA Ops:
  0.0 55.5 %copy-start = (bf16[1024,1024]{1,0:T(8,128)(2,1)S(1)}, bf16[1024,1024]{1,0:T(8,128)(2,1)}, u32[]{:S(2)}) copy-start(bf16[1024,1024]{1,0:T(8,128)(2,1)} %w_ref.2) | copy-start | bytes 6291460
  0.0 1.1 %copy-start.1 = (bf16[128,1024]{1,0:T(8,128)(2,1)S(1)}, bf16[128,1024]{1,0:T(8,128)(2,1)}, u32[]{:S(2)}) copy-start(bf16[128,1024]{1,0:T(8,128)(2,1)} %x_ref.3) | copy-start | bytes 786436
  1.1 35.8 %copy-start.2 = (s32[32]{0:T(128)S(1)}, s32[32]{0:T(128)}, u32[]{:S(2)}) copy-start(s32[32]{0:T(128)} %time_ref.1) | copy-start | bytes 388

commit v3 on v2

--- a/solution.py
+++ b/solution.py
@@ -16,9 +16,17 @@
 KTILE = 1024
 GROUP = 256
 CHUNK = 256
-PROJECT_VMEM = 52 * 2**20
+PROJECT_VMEM = 24 * 2**20
 NT = (((1,), (1,)), ((), ()))
 SCALE = 0.125 * 1.4426950408889634
+
+
+def in_hbm(array):
+    return pltpu.with_memory_space_constraint(array, pltpu.HBM)
+
+
+def in_vmem(array):
+    return pltpu.with_memory_space_constraint(array, pltpu.VMEM)
 
 
 def swap_halves(tile):
@@ -28,20 +36,23 @@
     return first, second
 
 
-def project_kernel(x_ref, w_ref, out_ref, w_buf, total, sem):
+def project_kernel(x_ref, w_ref, out_ref, x_buf, w_buf, total, sem):
     chunks = D // CHUNK
+    x_copy = pltpu.make_async_copy(x_ref, x_buf, sem.at[chunks])
+    x_copy.start()
     copies = []
     for c in range(chunks):
         rows = pl.ds(c * CHUNK, CHUNK)
         copies.append(pltpu.make_async_copy(w_ref.at[rows], w_buf.at[rows], sem.at[c]))
         copies[-1].start()
+    x_copy.wait()
     for c in range(chunks):
         copies[c].wait()
         depth = slice(c * CHUNK, (c + 1) * CHUNK)
         for g in range(3 * D // GROUP):
             columns = slice(g * GROUP, (g + 1) * GROUP)
             y = jnp.dot(
-                x_ref[:, depth], w_buf[depth, columns], preferred_element_type=jnp.float32
+                x_buf[:, depth], w_buf[depth, columns], preferred_element_type=jnp.float32
             )
             if c:
                 y = y + total[:, columns]
@@ -60,20 +71,18 @@
 def project(x, w):
     return pl.pallas_call(
         project_kernel,
-        out_shape=jax.ShapeDtypeStruct((HEADS, 3 * BLK, ROWS), jnp.bfloat16),
-        in_specs=[
-            pl.BlockSpec(memory_space=pltpu.VMEM),
-            pl.BlockSpec(memory_space=pl.ANY),
-        ],
+        out_shape=pltpu.VMEM((HEADS, 3 * BLK, ROWS), jnp.bfloat16),
+        in_specs=[pl.BlockSpec(memory_space=pl.ANY)] * 2,
         out_specs=pl.BlockSpec(memory_space=pltpu.VMEM),
         scratch_shapes=[
+            pltpu.VMEM((ROWS, D), jnp.bfloat16),
             pltpu.VMEM((D, 3 * D), jnp.bfloat16),
             pltpu.VMEM((ROWS, 3 * D), jnp.float32),
-            pltpu.SemaphoreType.DMA((D // CHUNK,)),
+            pltpu.SemaphoreType.DMA((D // CHUNK + 1,)),
         ],
         compiler_params=pltpu.CompilerParams(vmem_limit_bytes=PROJECT_VMEM),
         name="project",
-    )(x, w)
+    )(in_hbm(x), in_hbm(w))
 
 
 def attend_kernel(time_ref, in_ref, out_ref, qs, ks, vs, os):
@@ -116,7 +125,7 @@
 def attend(block_time, received):
     return pl.pallas_call(
         attend_kernel,
-        out_shape=jax.ShapeDtypeStruct((N_TM, BLK, ROWS), jnp.bfloat16),
+        out_shape=pltpu.VMEM((N_TM, BLK, ROWS), jnp.bfloat16),
         in_specs=[
             pl.BlockSpec(memory_space=pltpu.SMEM),
             pl.BlockSpec(memory_space=pltpu.VMEM),
@@ -130,7 +139,7 @@
         ],
         compiler_params=pltpu.CompilerParams(vmem_limit_bytes=32 * 2**20),
         name="attend",
-    )(block_time, received)
+    )(block_time, in_vmem(received))
 
 
 def mix_kernel(in_ref, x_ref, w_ref, out_ref, rows_ref):
@@ -152,12 +161,11 @@
         scratch_shapes=[pltpu.VMEM((ROWS, D), jnp.bfloat16)],
         compiler_params=pltpu.CompilerParams(vmem_limit_bytes=16 * 2**20),
         name="mix",
-    )(attended, x, w)
+    )(in_vmem(attended), in_vmem(x), in_vmem(w))
 
 
 def shards(series, block_time, w_qkv, w_out):
     sent = project(series, w_qkv)
-    sent, w_out = lax.optimization_barrier((sent, w_out))
     received = lax.all_to_all(sent, "tm", 0, 0, tiled=True)
     attended = attend(block_time, received)
     returned = lax.all_to_all(attended, "tm", 0, 0, tiled=True)

time: 56.9 us -> 56 us (0.984)
  local copies, waits for them, and re-layouts: 1.11 us -> 0.01 us
    unnamed x6, local copies, waits for them, and re-layouts: 1.11 us -> 0.01 us
where the time goes in v3:
time: 56 us; the launch traced here: 55.8 us
  blocking collectives  46.7 us (83%)
  Pallas kernels  9.11 us (16%)
    all_to_all x1, blocking collectives, shards(): received = lax.all_to_all(sent, 'tm', 0, 0, tiled=True)  32.5 us
    all_to_all x1, blocking collectives, shards(): returned = lax.all_to_all(attended, 'tm', 0, 0, tiled=True)  14.2 us
    pallas_call x1, Pallas kernels, attend(): pl.pallas_call(attend_kernel, out_shape=pltpu.VMEM((N_TM, BLK, ROWS), jnp...  4.34 us
    pallas_call x1, Pallas kernels, project(): pl.pallas_call(project_kernel, out_shape=pltpu.VMEM((HEADS, 3 * BLK, ROWS...  3.56 us
    pallas_call x1, Pallas kernels, mix(): pl.pallas_call(mix_kernel, out_shape=jax.ShapeDtypeStruct((ROWS, D), jnp....  1.22 us

profile of v3, /device:TPU:1, one launch (start us, length us, event | category | flops | bytes accessed | tf_op | source)
XLA Modules:
  0.0 55.8 jit_solution(11526740747015272627)
XLA Ops:
  0.0 0.0 copy-start.1
  0.0 0.0 copy-start.2
  0.0 0.0 copy-start
  0.0 3.6 %project.1 = bf16[16,192,128]{2,1,0:T(8,128)(2,1)S(1)} custom-call(bf16[128,1024]{1,0:T(8,128)(2,1)} %x_ref.3, bf16[1024,3072]{1,0:T(8,128)(2,1)} %w_ref.2), custom_call_target="tpu_custom_call" | custom-call | tf_op jit(solution)/shard_map/project/pallas_call | solution.py:72
  3.6 32.5 %all_to_all.10.in_ref = bf16[16,192,128]{2,1,0:T(8,128)(2,1)S(1)} all-to-all(bf16[16,192,128]{2,1,0:T(8,128)(2,1)S(1)} %project.1), channel_id=1, replica_groups=mesh['tm'=16,'clus'=32] {'tm'}, dimensions={0} | all-to-all | bytes 1572864 | tf_op jit(solution)/shard_map/all_to_all | solution.py:169
  36.0 0.0 copy-done.2
  36.0 4.3 %attend.1 = bf16[16,64,128]{2,1,0:T(8,128)(2,1)S(1)} custom-call(s32[32]{0:T(128)S(1)} %copy-done.2, bf16[16,192,128]{2,1,0:T(8,128)(2,1)S(1)} %all_to_all.10.in_ref), custom_call_target="tpu_custom_call" | custom-call | tf_op jit(solution)/shard_map/attend/pallas_call | solution.py:126
  40.4 14.2 %all_to_all.11.in_ref = bf16[16,64,128]{2,1,0:T(8,128)(2,1)S(1)} all-to-all(bf16[16,64,128]{2,1,0:T(8,128)(2,1)S(1)} %attend.1), channel_id=1, replica_groups=mesh['tm'=16,'clus'=32] {'tm'}, dimensions={0} | all-to-all | bytes 524288 | tf_op jit(solution)/shard_map/all_to_all | solution.py:171
  54.6 0.0 copy-done.1
  54.6 0.0 copy-done
  54.6 1.2 %mix.1 = bf16[128,1024]{1,0:T(8,128)(2,1)} custom-call(bf16[16,64,128]{2,1,0:T(8,128)(2,1)S(1)} %all_to_all.11.in_ref, bf16[128,1024]{1,0:T(8,128)(2,1)S(1)} %copy-done.1, bf16[1024,1024]{1,0:T(8,128)(2,1)S(1)} %copy-done), custom_call_target="tpu_custom_call" | custom-call | tf_op jit(solution)/shard_map/mix/pallas_call | solution.py:156
Async XLA Ops:
  0.0 54.6 %copy-start.1 = (bf16[128,1024]{1,0:T(8,128)(2,1)S(1)}, bf16[128,1024]{1,0:T(8,128)(2,1)}, u32[]{:S(2)}) copy-start(bf16[128,1024]{1,0:T(8,128)(2,1)} %x_ref.3) | copy-start | bytes 786436
  0.0 36.0 %copy-start.2 = (s32[32]{0:T(128)S(1)}, s32[32]{0:T(128)}, u32[]{:S(2)}) copy-start(s32[32]{0:T(128)} %time_ref.1) | copy-start | bytes 388
  0.0 54.6 %copy-start = (bf16[1024,1024]{1,0:T(8,128)(2,1)S(1)}, bf16[1024,1024]{1,0:T(8,128)(2,1)}, u32[]{:S(2)}) copy-start(bf16[1024,1024]{1,0:T(8,128)(2,1)} %w_ref.3) | copy-start | bytes 6291460

commit v4 on v3

--- a/solution.py
+++ b/solution.py
@@ -36,15 +36,17 @@
     return first, second
 
 
-def project_kernel(x_ref, w_ref, out_ref, x_buf, w_buf, total, sem):
+def project_kernel(x_ref, w_ref, time_ref, out_ref, time_out, x_buf, w_buf, total, sem):
     chunks = D // CHUNK
     x_copy = pltpu.make_async_copy(x_ref, x_buf, sem.at[chunks])
     x_copy.start()
+    time_copy = pltpu.make_async_copy(time_ref, time_out, sem.at[chunks + 1])
     copies = []
     for c in range(chunks):
         rows = pl.ds(c * CHUNK, CHUNK)
         copies.append(pltpu.make_async_copy(w_ref.at[rows], w_buf.at[rows], sem.at[c]))
         copies[-1].start()
+    time_copy.start()
     x_copy.wait()
     for c in range(chunks):
         copies[c].wait()
@@ -66,23 +68,27 @@
                 head = start // HEAD + 2 * pair
                 out_ref[head, part * BLK : part * BLK + BLK, :] = first
                 out_ref[head + 1, part * BLK : part * BLK + BLK, :] = second
+    time_copy.wait()
 
 
-def project(x, w):
+def project(x, w, block_time):
     return pl.pallas_call(
         project_kernel,
-        out_shape=pltpu.VMEM((HEADS, 3 * BLK, ROWS), jnp.bfloat16),
-        in_specs=[pl.BlockSpec(memory_space=pl.ANY)] * 2,
-        out_specs=pl.BlockSpec(memory_space=pltpu.VMEM),
+        out_shape=[
+            pltpu.VMEM((HEADS, 3 * BLK, ROWS), jnp.bfloat16),
+            pltpu.SMEM((2 * N_TM,), jnp.int32),
+        ],
+        in_specs=[pl.BlockSpec(memory_space=pl.ANY)] * 3,
+        out_specs=[pl.BlockSpec(memory_space=pltpu.VMEM), pl.BlockSpec(memory_space=pltpu.SMEM)],
         scratch_shapes=[
             pltpu.VMEM((ROWS, D), jnp.bfloat16),
             pltpu.VMEM((D, 3 * D), jnp.bfloat16),
             pltpu.VMEM((ROWS, 3 * D), jnp.float32),
-            pltpu.SemaphoreType.DMA((D // CHUNK + 1,)),
+            pltpu.SemaphoreType.DMA((D // CHUNK + 2,)),
         ],
         compiler_params=pltpu.CompilerParams(vmem_limit_bytes=PROJECT_VMEM),
         name="project",
-    )(in_hbm(x), in_hbm(w))
+    )(in_hbm(x), in_hbm(w), in_hbm(block_time))
 
 
 def attend_kernel(time_ref, in_ref, out_ref, qs, ks, vs, os):
@@ -139,7 +145,7 @@
         ],
         compiler_params=pltpu.CompilerParams(vmem_limit_bytes=32 * 2**20),
         name="attend",
-    )(block_time, in_vmem(received))
+    )(pltpu.with_memory_space_constraint(block_time, pltpu.SMEM), in_vmem(received))
 
 
 def mix_kernel(in_ref, x_ref, w_ref, out_ref, rows_ref):
@@ -165,9 +171,9 @@
 
 
 def shards(series, block_time, w_qkv, w_out):
-    sent = project(series, w_qkv)
+    sent, times = project(series, w_qkv, block_time)
     received = lax.all_to_all(sent, "tm", 0, 0, tiled=True)
-    attended = attend(block_time, received)
+    attended = attend(times, received)
     returned = lax.all_to_all(attended, "tm", 0, 0, tiled=True)
     return mix(returned, series, w_out)
 

time: 56 us -> 55.4 us (0.989)
  no operation moved by 1% of the time
where the time goes in v4:
time: 55.4 us; the launch traced here: 55.3 us
  blocking collectives  46.7 us (84%)
  Pallas kernels  8.57 us (15%)
    all_to_all x1, blocking collectives, shards(): received = lax.all_to_all(sent, 'tm', 0, 0, tiled=True)  32.5 us
    all_to_all x1, blocking collectives, shards(): returned = lax.all_to_all(attended, 'tm', 0, 0, tiled=True)  14.2 us
    pallas_call x1, Pallas kernels, attend(): pl.pallas_call(attend_kernel, out_shape=pltpu.VMEM((N_TM, BLK, ROWS), jnp...  3.79 us
    pallas_call x1, Pallas kernels, project(): pl.pallas_call(project_kernel, out_shape=[pltpu.VMEM((HEADS, 3 * BLK, ROW...  3.58 us
    pallas_call x1, Pallas kernels, mix(): pl.pallas_call(mix_kernel, out_shape=jax.ShapeDtypeStruct((ROWS, D), jnp....  1.2 us

profile of v4, /device:TPU:1, one launch (start us, length us, event | category | flops | bytes accessed | tf_op | source)
XLA Modules:
  0.0 55.3 jit_solution(9155057637788859780)
XLA Ops:
  0.0 0.0 copy-start.1
  0.0 0.0 copy-start
  0.0 3.6 %project.1 = (bf16[16,192,128]{2,1,0:T(8,128)(2,1)S(1)}, s32[32]{0:T(128)S(4)}) custom-call(bf16[128,1024]{1,0:T(8,128)(2,1)} %x_ref.3, bf16[1024,3072]{1,0:T(8,128)(2,1)} %w_ref.2, s32[32]{0:T(128)} %time_ref.1), custom_call_target="tpu_custom_call" | custom-call | tf_op jit(solution)/shard_map/project/pallas_call | solution.py:75
  3.6 32.5 %all_to_all.10.in_ref = bf16[16,192,128]{2,1,0:T(8,128)(2,1)S(1)} all-to-all(bf16[16,192,128]{2,1,0:T(8,128)(2,1)S(1)} %get-tuple-element.8), channel_id=1, replica_groups=mesh['tm'=16,'clus'=32] {'tm'}, dimensions={0} | all-to-all | bytes 1572864 | tf_op jit(solution)/shard_map/all_to_all | solution.py:175
  36.1 3.8 %attend.1 = bf16[16,64,128]{2,1,0:T(8,128)(2,1)S(1)} custom-call(s32[32]{0:T(128)S(4)} %get-tuple-element.7.time_ref, bf16[16,192,128]{2,1,0:T(8,128)(2,1)S(1)} %all_to_all.10.in_ref), custom_call_target="tpu_custom_call" | custom-call | tf_op jit(solution)/shard_map/attend/pallas_call | solution.py:132
  39.8 14.2 %all_to_all.11.in_ref = bf16[16,64,128]{2,1,0:T(8,128)(2,1)S(1)} all-to-all(bf16[16,64,128]{2,1,0:T(8,128)(2,1)S(1)} %attend.1), channel_id=1, replica_groups=mesh['tm'=16,'clus'=32] {'tm'}, dimensions={0} | all-to-all | bytes 524288 | tf_op jit(solution)/shard_map/all_to_all | solution.py:177
  54.1 0.0 copy-done.1
  54.1 0.0 copy-done
  54.1 1.2 %mix.1 = bf16[128,1024]{1,0:T(8,128)(2,1)} custom-call(bf16[16,64,128]{2,1,0:T(8,128)(2,1)S(1)} %all_to_all.11.in_ref, bf16[128,1024]{1,0:T(8,128)(2,1)S(1)} %copy-done.1, bf16[1024,1024]{1,0:T(8,128)(2,1)S(1)} %copy-done), custom_call_target="tpu_custom_call" | custom-call | tf_op jit(solution)/shard_map/mix/pallas_call | solution.py:162
Async XLA Ops:
  0.0 54.1 %copy-start.1 = (bf16[128,1024]{1,0:T(8,128)(2,1)S(1)}, bf16[128,1024]{1,0:T(8,128)(2,1)}, u32[]{:S(2)}) copy-start(bf16[128,1024]{1,0:T(8,128)(2,1)} %x_ref.3) | copy-start | bytes 786436
  0.0 54.1 %copy-start = (bf16[1024,1024]{1,0:T(8,128)(2,1)S(1)}, bf16[1024,1024]{1,0:T(8,128)(2,1)}, u32[]{:S(2)}) copy-start(bf16[1024,1024]{1,0:T(8,128)(2,1)} %w_ref.3) | copy-start | bytes 6291460

commit v5 on v4

--- a/solution.py
+++ b/solution.py
@@ -51,23 +51,28 @@
     for c in range(chunks):
         copies[c].wait()
         depth = slice(c * CHUNK, (c + 1) * CHUNK)
-        for g in range(3 * D // GROUP):
-            columns = slice(g * GROUP, (g + 1) * GROUP)
-            y = jnp.dot(
-                x_buf[:, depth], w_buf[depth, columns], preferred_element_type=jnp.float32
-            )
-            if c:
-                y = y + total[:, columns]
+        for g in range(D // GROUP):
+            parts = []
+            for part in range(3):
+                columns = slice(part * D + g * GROUP, part * D + (g + 1) * GROUP)
+                y = jnp.dot(
+                    x_buf[:, depth], w_buf[depth, columns], preferred_element_type=jnp.float32
+                )
+                if c:
+                    y = y + total[:, columns]
+                if c < chunks - 1:
+                    total[:, columns] = y
+                parts.append(y.astype(jnp.bfloat16))
             if c < chunks - 1:
-                total[:, columns] = y
                 continue
-            y = y.astype(jnp.bfloat16)
-            part, start = g * GROUP // D, g * GROUP % D
             for pair in range(GROUP // 128):
-                first, second = swap_halves(y[:, pair * 128 : pair * 128 + 128])
-                head = start // HEAD + 2 * pair
-                out_ref[head, part * BLK : part * BLK + BLK, :] = first
-                out_ref[head + 1, part * BLK : part * BLK + BLK, :] = second
+                q, k, v = (y[:, pair * 128 : pair * 128 + 128] for y in parts)
+                head = g * GROUP // HEAD + 2 * pair
+                first, second = swap_halves(k)
+                out_ref[head, :ROWS, :] = jnp.concatenate([q[:, :HEAD], v[:, :HEAD]], axis=1)
+                out_ref[head, ROWS:, :] = first
+                out_ref[head + 1, :ROWS, :] = jnp.concatenate([q[:, HEAD:], v[:, HEAD:]], axis=1)
+                out_ref[head + 1, ROWS:, :] = second
     time_copy.wait()
 
 
@@ -92,14 +97,17 @@
 
 
 def attend_kernel(time_ref, in_ref, out_ref, qs, ks, vs, os):
-    ones = jnp.ones((BLK, HEAD), jnp.bfloat16)
+    lower = lax.broadcasted_iota(jnp.int32, (BLK, ROWS), 1) < HEAD
     for b in range(2 * N_TM):
         source, half = b // 2, b % 2
         rows = pl.ds(pl.multiple_of(time_ref[b] * BLK, BLK), BLK)
-        columns = slice(half * HEAD, half * HEAD + HEAD)
-        qs[rows, :] = in_ref[source, :BLK, columns]
-        ks[rows, :] = in_ref[source, BLK : 2 * BLK, columns]
-        vs[rows, :] = jnp.concatenate([in_ref[source, 2 * BLK :, columns], ones], axis=1)
+        both = in_ref[source, half * BLK : half * BLK + BLK, :]
+        keys = in_ref[source, ROWS:, :]
+        if half:
+            keys = jnp.concatenate([keys[:, HEAD:], keys[:, :HEAD]], axis=1)
+        qs[rows, :] = jnp.where(lower, both, jnp.zeros_like(both))
+        ks[rows, :] = keys
+        vs[rows, :] = jnp.where(lower, jnp.ones_like(both), both)
     for start in range(0, TOKENS, QTILE):
         q = qs[start : start + QTILE, :]
         top = summed = None
@@ -119,12 +127,13 @@
             if top is not None:
                 added = summed * jnp.exp2((top - new_top) * SCALE) + added
             top, summed = new_top, added
-        os[start : start + QTILE, :] = (summed[:, :HEAD] / summed[:, HEAD:]).astype(jnp.bfloat16)
+        totals = jnp.concatenate([summed[:, HEAD:], summed[:, :HEAD]], axis=1)
+        os[start : start + QTILE, :] = (summed / totals).astype(jnp.bfloat16)
     for s in range(N_TM):
         pair = []
         for half in range(2):
             rows = pl.ds(pl.multiple_of(time_ref[2 * s + half] * BLK, BLK), BLK)
-            pair.append(os[rows, :])
+            pair.append(os[rows, HEAD:])
         out_ref[s] = jnp.concatenate(pair, axis=1)
 
 
@@ -138,10 +147,10 @@
         ],
         out_specs=pl.BlockSpec(memory_space=pltpu.VMEM),
         scratch_shapes=[
-            pltpu.VMEM((TOKENS, HEAD), jnp.bfloat16),
-            pltpu.VMEM((TOKENS, HEAD), jnp.bfloat16),
             pltpu.VMEM((TOKENS, 2 * HEAD), jnp.bfloat16),
-            pltpu.VMEM((TOKENS, HEAD), jnp.bfloat16),
+            pltpu.VMEM((TOKENS, 2 * HEAD), jnp.bfloat16),
+            pltpu.VMEM((TOKENS, 2 * HEAD), jnp.bfloat16),
+            pltpu.VMEM((TOKENS, 2 * HEAD), jnp.bfloat16),
         ],
         compiler_params=pltpu.CompilerParams(vmem_limit_bytes=32 * 2**20),
         name="attend",

time: 55.4 us -> 55.4 us (level)
  no operation moved by 1% of the time
where the time goes in v5:
time: 55.4 us; the launch traced here: 55.3 us
  blocking collectives  46.7 us (84%)
  Pallas kernels  8.54 us (15%)
    all_to_all x1, blocking collectives, shards(): received = lax.all_to_all(sent, 'tm', 0, 0, tiled=True)  32.5 us
    all_to_all x1, blocking collectives, shards(): returned = lax.all_to_all(attended, 'tm', 0, 0, tiled=True)  14.2 us
    pallas_call x1, Pallas kernels, attend(): pl.pallas_call(attend_kernel, out_shape=pltpu.VMEM((N_TM, BLK, ROWS), jnp...  3.77 us
    pallas_call x1, Pallas kernels, project(): pl.pallas_call(project_kernel, out_shape=[pltpu.VMEM((HEADS, 3 * BLK, ROW...  3.57 us
    pallas_call x1, Pallas kernels, mix(): pl.pallas_call(mix_kernel, out_shape=jax.ShapeDtypeStruct((ROWS, D), jnp....  1.2 us

profile of v5, /device:TPU:1, one launch (start us, length us, event | category | flops | bytes accessed | tf_op | source)
XLA Modules:
  0.0 55.3 jit_solution(2026897983513101422)
XLA Ops:
  0.0 0.0 copy-start.1
  0.0 0.0 copy-start
  0.0 3.6 %project.1 = (bf16[16,192,128]{2,1,0:T(8,128)(2,1)S(1)}, s32[32]{0:T(128)S(4)}) custom-call(bf16[128,1024]{1,0:T(8,128)(2,1)} %x_ref.3, bf16[1024,3072]{1,0:T(8,128)(2,1)} %w_ref.2, s32[32]{0:T(128)} %time_ref.1), custom_call_target="tpu_custom_call" | custom-call | tf_op jit(solution)/shard_map/project/pallas_call | solution.py:80
  3.6 32.5 %all_to_all.10.in_ref = bf16[16,192,128]{2,1,0:T(8,128)(2,1)S(1)} all-to-all(bf16[16,192,128]{2,1,0:T(8,128)(2,1)S(1)} %get-tuple-element.8), channel_id=1, replica_groups=mesh['tm'=16,'clus'=32] {'tm'}, dimensions={0} | all-to-all | bytes 1572864 | tf_op jit(solution)/shard_map/all_to_all | solution.py:184
  36.1 3.8 %attend.1 = bf16[16,64,128]{2,1,0:T(8,128)(2,1)S(1)} custom-call(s32[32]{0:T(128)S(4)} %get-tuple-element.7.time_ref, bf16[16,192,128]{2,1,0:T(8,128)(2,1)S(1)} %all_to_all.10.in_ref), custom_call_target="tpu_custom_call" | custom-call | tf_op jit(solution)/shard_map/attend/pallas_call | solution.py:141
  39.8 14.2 %all_to_all.11.in_ref = bf16[16,64,128]{2,1,0:T(8,128)(2,1)S(1)} all-to-all(bf16[16,64,128]{2,1,0:T(8,128)(2,1)S(1)} %attend.1), channel_id=1, replica_groups=mesh['tm'=16,'clus'=32] {'tm'}, dimensions={0} | all-to-all | bytes 524288 | tf_op jit(solution)/shard_map/all_to_all | solution.py:186
  54.0 0.0 copy-done.1
  54.1 0.0 copy-done
  54.1 1.2 %mix.1 = bf16[128,1024]{1,0:T(8,128)(2,1)} custom-call(bf16[16,64,128]{2,1,0:T(8,128)(2,1)S(1)} %all_to_all.11.in_ref, bf16[128,1024]{1,0:T(8,128)(2,1)S(1)} %copy-done.1, bf16[1024,1024]{1,0:T(8,128)(2,1)S(1)} %copy-done), custom_call_target="tpu_custom_call" | custom-call | tf_op jit(solution)/shard_map/mix/pallas_call | solution.py:171
Async XLA Ops:
  0.0 54.1 %copy-start.1 = (bf16[128,1024]{1,0:T(8,128)(2,1)S(1)}, bf16[128,1024]{1,0:T(8,128)(2,1)}, u32[]{:S(2)}) copy-start(bf16[128,1024]{1,0:T(8,128)(2,1)} %x_ref.3) | copy-start | bytes 786436
  0.0 54.1 %copy-start = (bf16[1024,1024]{1,0:T(8,128)(2,1)S(1)}, bf16[1024,1024]{1,0:T(8,128)(2,1)}, u32[]{:S(2)}) copy-start(bf16[1024,1024]{1,0:T(8,128)(2,1)} %w_ref.3) | copy-start | bytes 6291460

commit v6 on v4

--- a/solution.py
+++ b/solution.py
@@ -15,7 +15,7 @@
 QTILE = 512
 KTILE = 1024
 GROUP = 256
-CHUNK = 256
+CHUNK = 128
 PROJECT_VMEM = 24 * 2**20
 NT = (((1,), (1,)), ((), ()))
 SCALE = 0.125 * 1.4426950408889634

time: 55.4 us -> 55.4 us (level)
  no operation moved by 1% of the time
where the time goes in v6:
time: 55.4 us; the launch traced here: 55.3 us
  blocking collectives  46.7 us (84%)
  Pallas kernels  8.56 us (15%)
    all_to_all x1, blocking collectives, shards(): received = lax.all_to_all(sent, 'tm', 0, 0, tiled=True)  32.5 us
    all_to_all x1, blocking collectives, shards(): returned = lax.all_to_all(attended, 'tm', 0, 0, tiled=True)  14.2 us
    pallas_call x1, Pallas kernels, attend(): pl.pallas_call(attend_kernel, out_shape=pltpu.VMEM((N_TM, BLK, ROWS), jnp...  3.79 us
    pallas_call x1, Pallas kernels, project(): pl.pallas_call(project_kernel, out_shape=[pltpu.VMEM((HEADS, 3 * BLK, ROW...  3.57 us
    pallas_call x1, Pallas kernels, mix(): pl.pallas_call(mix_kernel, out_shape=jax.ShapeDtypeStruct((ROWS, D), jnp....  1.2 us

profile of v6, /device:TPU:1, one launch (start us, length us, event | category | flops | bytes accessed | tf_op | source)
XLA Modules:
  0.0 55.3 jit_solution(2447998371093949636)
XLA Ops:
  0.0 0.0 copy-start.1
  0.0 0.0 copy-start
  0.0 3.6 %project.1 = (bf16[16,192,128]{2,1,0:T(8,128)(2,1)S(1)}, s32[32]{0:T(128)S(4)}) custom-call(bf16[128,1024]{1,0:T(8,128)(2,1)} %x_ref.3, bf16[1024,3072]{1,0:T(8,128)(2,1)} %w_ref.2, s32[32]{0:T(128)} %time_ref.1), custom_call_target="tpu_custom_call" | custom-call | tf_op jit(solution)/shard_map/project/pallas_call | solution.py:75
  3.6 32.5 %all_to_all.10.in_ref = bf16[16,192,128]{2,1,0:T(8,128)(2,1)S(1)} all-to-all(bf16[16,192,128]{2,1,0:T(8,128)(2,1)S(1)} %get-tuple-element.8), channel_id=1, replica_groups=mesh['tm'=16,'clus'=32] {'tm'}, dimensions={0} | all-to-all | bytes 1572864 | tf_op jit(solution)/shard_map/all_to_all | solution.py:175
  36.0 3.8 %attend.1 = bf16[16,64,128]{2,1,0:T(8,128)(2,1)S(1)} custom-call(s32[32]{0:T(128)S(4)} %get-tuple-element.7.time_ref, bf16[16,192,128]{2,1,0:T(8,128)(2,1)S(1)} %all_to_all.10.in_ref), custom_call_target="tpu_custom_call" | custom-call | tf_op jit(solution)/shard_map/attend/pallas_call | solution.py:132
  39.8 14.2 %all_to_all.11.in_ref = bf16[16,64,128]{2,1,0:T(8,128)(2,1)S(1)} all-to-all(bf16[16,64,128]{2,1,0:T(8,128)(2,1)S(1)} %attend.1), channel_id=1, replica_groups=mesh['tm'=16,'clus'=32] {'tm'}, dimensions={0} | all-to-all | bytes 524288 | tf_op jit(solution)/shard_map/all_to_all | solution.py:177
  54.1 0.0 copy-done.1
  54.1 0.0 copy-done
  54.1 1.2 %mix.1 = bf16[128,1024]{1,0:T(8,128)(2,1)} custom-call(bf16[16,64,128]{2,1,0:T(8,128)(2,1)S(1)} %all_to_all.11.in_ref, bf16[128,1024]{1,0:T(8,128)(2,1)S(1)} %copy-done.1, bf16[1024,1024]{1,0:T(8,128)(2,1)S(1)} %copy-done), custom_call_target="tpu_custom_call" | custom-call | tf_op jit(solution)/shard_map/mix/pallas_call | solution.py:162
Async XLA Ops:
  0.0 54.1 %copy-start.1 = (bf16[128,1024]{1,0:T(8,128)(2,1)S(1)}, bf16[128,1024]{1,0:T(8,128)(2,1)}, u32[]{:S(2)}) copy-start(bf16[128,1024]{1,0:T(8,128)(2,1)} %x_ref.3) | copy-start | bytes 786436
  0.0 54.1 %copy-start = (bf16[1024,1024]{1,0:T(8,128)(2,1)S(1)}, bf16[1024,1024]{1,0:T(8,128)(2,1)}, u32[]{:S(2)}) copy-start(bf16[1024,1024]{1,0:T(8,128)(2,1)} %w_ref.3) | copy-start | bytes 6291460
